TPU v7x, 256 devices: a whole 4x4x8 slice. The times are simulated.
256 devices in a mesh: variant: 8 (over x, core), mesh: 32 (over z, y).
Axes of the slice: x: 4, y: 4, z: 8, core: 2. Of those that a mesh axis runs over, the one named last changes fastest.
Arguments:
- snapshots: float32 [8, 64, 524288], P('variant', None, 'mesh'), may hold values from -12 to 12, as said below
- ref_index: int32 [1], replicated, may hold values from 0 to 7
- weight_codes: int32 [8], replicated, may hold values from 1 to 16
Outputs:
- new_basis: float32 [64, 524288], P(None, 'mesh')
Inputs may be any that keep to these rules, and one draw needn't show every extreme that they name: `snapshots`: each variant's snapshot matrix has full rank 64, and the principal angles between any two variants' spans have tangents below 0.8.
All inputs are finite; a program needn't handle non-finite values.
Results may differ from a plain program's by a relative error of at most 0.0001.
Values sent between devices are 32-bit elements; how exact they have to be, the bound alone decides.
A program may use at most 64 MiB of HBM per device.

v0:
```python
import math

import jax
import jax.numpy as jnp
from jax import lax
from jax.sharding import Mesh
from jax.sharding import PartitionSpec as P

VARIANT = ("variant_0", "variant_1")


highest = lax.Precision.HIGHEST
atan_coeffs = [(-1.0) ** k / (2 * k + 1) for k in range(24)]
cos_coeffs = [(-1.0) ** k / math.factorial(2 * k) for k in range(24)]
sin_coeffs = [(-1.0) ** k / math.factorial(2 * k + 1) for k in range(24)]


def from_everyone(x, axis):
    count = lax.axis_size(axis)
    return lax.all_to_all(jnp.broadcast_to(x[None], (count, *x.shape)), axis, 0, 0, tiled=True)


def of_everyone(x, axis):
    everything = from_everyone(x, axis)
    return jnp.sum(everything, axis=0)


def spread(x, axes, root):
    x = jnp.where(lax.axis_index(axes) == root, x, jnp.zeros_like(x))
    for axis in axes:
        x = lax.psum(x, axis)
    return x


def product(left, right):
    return jnp.dot(left, right, precision=highest, preferred_element_type=jnp.float32)


def series(matrix, coeffs):
    eye = jnp.eye(matrix.shape[0], dtype=jnp.float32)
    total = coeffs[-1] * eye
    for coeff in reversed(coeffs[:-1]):
        total = coeff * eye + product(matrix, total)
    return total


def inverse(matrix):
    factor = jnp.linalg.cholesky(product(matrix.T, matrix))
    return jax.scipy.linalg.cho_solve((factor, True), matrix.T)


def on_device(snapshots, ref_index, weight_codes):
    own_snap = snapshots[0]
    root = ref_index[0]
    codes = weight_codes.astype(jnp.float32)
    weight = codes[lax.axis_index(VARIANT)] / jnp.sum(codes)
    eye = jnp.eye(own_snap.shape[0], dtype=jnp.float32)
    scale = jnp.float32(math.sqrt(own_snap.shape[1] * lax.axis_size("mesh")))
    gram_own = of_everyone(product(own_snap, own_snap.T), "mesh")
    lower_own = jnp.linalg.cholesky(gram_own)
    base_own = jax.scipy.linalg.solve_triangular(lower_own, own_snap, lower=True)
    base_ref = spread(base_own, VARIANT, root)
    correlation = of_everyone(product(base_ref, base_own.T), "mesh")
    minv = inverse(correlation)
    tangent = product(minv.T, base_own) - base_ref
    tangent_gram = product(minv.T, minv) - eye
    term = weight * product(series(tangent_gram, atan_coeffs), tangent)
    blended = lax.psum(term, VARIANT)
    energy = of_everyone(product(blended, blended.T), "mesh")
    mixed = product(series(energy, cos_coeffs), base_ref) + product(
        series(energy, sin_coeffs), blended
    )
    return mixed * scale


def solution(mesh):
    finer = Mesh(mesh.devices.reshape(4, 2, mesh.shape["mesh"]), ("variant_0", "variant_1", "mesh"))
    placed = (P(VARIANT, None, "mesh"), P(), P())
    return jax.shard_map(
        on_device, mesh=finer, in_specs=placed, out_specs=P(None, "mesh"), check_vma=False
    )
```

profile of v0, /device:TPU:1, one launch (start us, length us, event | category | flops | bytes accessed | tf_op | source)
XLA Modules:
  0.0 405.2 jit_solution(8007824990110213597)
XLA Ops:
  6.5 6.9 %fusion.3 = f32[64,64]{1,0:T(8,128)S(1)} fusion(f32[1,64,16384]{2,1,0:T(8,128)} %param.4), kind=kOutput, calls=%fused_computation.6 | convolution fusion | flops 805306368 | bytes 4210688 | tf_op jit(solution)/shard_map/dot_general | solution.py:36
  13.6 1.4 reshape.19
  15.0 12.0 %all-to-all-start = ((f32[32,1,4096]{2,1,0:T(1,128)}), f32[32,1,4096]{2,1,0:T(1,128)S(1)}, u32[]{:S(2)}, u32[]{:S(2)}) async-start(f32[32,1,4096]{2,1,0:T(1,128)} %reshape.19), calls=%async_computation | async-start | bytes 1048576 | tf_op jit(solution)/shard_map/all_to_all | solution.py:20
  28.1 15.3 %all-to-all-done = f32[32,1,4096]{2,1,0:T(1,128)S(1)} async-done(((f32[32,1,4096]{2,1,0:T(1,128)}), f32[32,1,4096]{2,1,0:T(1,128)S(1)}, u32[]{:S(2)}, u32[]{:S(2)}) %all-to-all-start) | async-done | bytes 524320 | tf_op jit(solution)/shard_map/all_to_all | solution.py:20
  43.9 1.9 reduce.4
  46.4 5.8 %cholesky.44 = f32[64,64]{1,0:T(8,128)S(1)} custom-call(f32[64,64]{1,0:T(8,128)S(1)} %fusion.15), custom_call_target="Cholesky" | custom-call | tf_op jit(solution)/shard_map/jit(cholesky)/cholesky | solution.py:60
  53.6 4.9 %custom-call.13 = f32[1,64,64]{1,2,0:T(8,128)S(1)} custom-call(f32[1,64,64]{2,1,0:T(8,128)S(1)} %fusion.7), custom_call_target="InvertDiagBlocksLowerTriangular" | custom-call | tf_op jit(solution)/shard_map/jit(_solve_triangular)/triangular_solve | solution.py:61
  58.5 9.3 %broadcast_select_fusion = (f32[64,16384]{1,0:T(8,128)}, f32[64,16384]{1,0:T(8,128)}) fusion(pred[]{:T(512)S(6)} %eq.142, f32[1,64,16384]{2,1,0:T(8,128)} %param.4, f32[1,64,64]{1,2,0:T(8,128)S(1)} %custom-call.13), kind=kOutput, calls=%fused_computation.8 | convolution fusion | flops 806354944 | bytes 12599297 | tf_op jit(solution)/shard_map/jit(_solve_triangular)/triangular_solve | solution.py:61
  67.8 95.9 %all-reduce.4.cloned.1.call-done = f32[64,16384]{1,0:T(8,128)} async-done(((f32[64,16384]{1,0:T(8,128)}), f32[64,16384]{1,0:T(8,128)}) %all-reduce.4.cloned.1.call-update) | async-done | bytes 4194320 | tf_op jit(solution)/shard_map/psum | solution.py:31
  163.7 42.8 %all-reduce.6.cloned.1.call-done = f32[64,16384]{1,0:T(8,128)} async-done(((f32[64,16384]{1,0:T(8,128)}), f32[64,16384]{1,0:T(8,128)}) %all-reduce.6.cloned.1.call-update) | async-done | bytes 4194320 | tf_op jit(solution)/shard_map/psum | solution.py:31
  206.6 6.9 %fusion.35 = f32[64,64]{1,0:T(8,128)S(1)} fusion(f32[64,16384]{1,0:T(8,128)} %all-reduce.6.cloned.1.call-done, f32[64,16384]{1,0:T(8,128)} %get-tuple-element.7), kind=kOutput, calls=%fused_computation.114 | convolution fusion | flops 805306368 | bytes 8404992 | tf_op jit(solution)/shard_map/dot_general | solution.py:36
  215.1 9.3 %all-to-all-start.1 = ((f32[32,1,4096]{2,1,0:T(1,128)}), f32[32,1,4096]{2,1,0:T(1,128)S(1)}, u32[]{:S(2)}, u32[]{:S(2)}) async-start(f32[32,1,4096]{2,1,0:T(1,128)} %reshape.21), calls=%async_computation.1 | async-start | bytes 1048576 | tf_op jit(solution)/shard_map/all_to_all | solution.py:20
  226.9 14.2 %all-to-all-done.1 = f32[32,1,4096]{2,1,0:T(1,128)S(1)} async-done(((f32[32,1,4096]{2,1,0:T(1,128)}), f32[32,1,4096]{2,1,0:T(1,128)S(1)}, u32[]{:S(2)}, u32[]{:S(2)}) %all-to-all-start.1) | async-done | bytes 524320 | tf_op jit(solution)/shard_map/all_to_all | solution.py:20
  241.1 1.9 reduce.5
  243.8 5.8 %cholesky.55 = f32[64,64]{1,0:T(8,128)S(1)} custom-call(f32[64,64]{1,0:T(8,128)S(1)} %fusion.13), custom_call_target="Cholesky" | custom-call | tf_op jit(solution)/shard_map/jit(cholesky)/cholesky | solution.py:48
  251.0 4.9 %custom-call.14 = f32[1,64,64]{1,2,0:T(8,128)S(1)} custom-call(f32[1,64,64]{2,1,0:T(8,128)S(1)} %fusion.8), custom_call_target="InvertDiagBlocksLowerTriangular" | custom-call | tf_op jit(solution)/shard_map/jit(_cho_solve)/triangular_solve | solution.py:49
  260.5 7.2 %convolution_subtract_fusion = f32[64,16384]{1,0:T(8,128)S(1)} fusion(f32[64,16384]{1,0:T(8,128)} %all-reduce.6.cloned.1.call-done, f32[64,64]{1,0:T(8,128)S(1)} %fusion.9, f32[64,16384]{1,0:T(8,128)} %get-tuple-element.7), kind=kOutput, calls=%fused_computation.3 | convolution fusion | flops 806354944 | bytes 12599296 | tf_op jit(solution)/shard_map/dot_general | solution.py:36
  267.6 5.4 %convolution_multiply_fusion = f32[64,16384]{1,0:T(8,128)} fusion(f32[64,64]{1,0:T(8,128)S(1)} %convolution_add_fusion.40, f32[64,16384]{1,0:T(8,128)S(1)} %convolution_subtract_fusion, f32[]{:T(128)S(6)} %div.9), kind=kOutput, calls=%fused_computation.2 | convolution fusion | flops 806354944 | bytes 8404996 | tf_op jit(solution)/shard_map/dot_general | solution.py:36
  273.1 73.5 %all-reduce.8.cloned.1.call-done = f32[64,16384]{1,0:T(8,128)} async-done(((f32[64,16384]{1,0:T(8,128)}), f32[64,16384]{1,0:T(8,128)}) %all-reduce.8.cloned.1.call-update) | async-done | bytes 4194320 | tf_op jit(solution)/shard_map/psum | solution.py:68
  346.5 6.9 %fusion.37 = f32[64,64]{1,0:T(8,128)S(1)} fusion(f32[64,16384]{1,0:T(8,128)} %all-reduce.8.cloned.1.call-done), kind=kOutput, calls=%fused_computation.116 | convolution fusion | flops 805306368 | bytes 4210688 | tf_op jit(solution)/shard_map/dot_general | solution.py:36
  354.2 23.7 %all_to_all.15 = f32[32,1,4096]{2,1,0:T(1,128)S(1)} all-to-all(f32[32,1,4096]{2,1,0:T(1,128)S(1)} %reshape.23), channel_id=1, replica_groups=mesh['variant_0'=4,'variant_1'=2,'mesh'=32] {'mesh'}, dimensions={0} | all-to-all | bytes 1048576 | tf_op jit(solution)/shard_map/all_to_all | solution.py:20
  377.9 1.9 reduce.6
  387.4 5.6 %fusion.40 = f32[64,16384]{1,0:T(8,128)S(1)} fusion(f32[64,64]{1,0:T(8,128)S(1)} %convolution_add_fusion.20, f32[64,16384]{1,0:T(8,128)} %all-reduce.6.cloned.1.call-done), kind=kOutput, calls=%fused_computation.119 | convolution fusion | flops 805306368 | bytes 8404992 | tf_op jit(solution)/shard_map/dot_general | solution.py:36
  393.1 5.4 %fusion = f32[64,16384]{1,0:T(8,128)} fusion(f32[64,16384]{1,0:T(8,128)S(1)} %fusion.40, f32[64,64]{1,0:T(8,128)S(1)} %convolution_add_fusion.1, f32[64,16384]{1,0:T(8,128)S(1)} %copy-done), kind=kOutput, calls=%fused_computation.1 | convolution fusion | flops 807403520 | bytes 12599296 | tf_op jit(solution)/shard_map/dot_general | solution.py:36
  (104 shorter events, 20.4 us)
Async XLA Ops:
  15.0 28.3 %all-to-all-start = ((f32[32,1,4096]{2,1,0:T(1,128)}), f32[32,1,4096]{2,1,0:T(1,128)S(1)}, u32[]{:S(2)}, u32[]{:S(2)}) async-start(f32[32,1,4096]{2,1,0:T(1,128)} %reshape.19), calls=%async_computation | async-start | bytes 1048576 | tf_op jit(solution)/shard_map/all_to_all | solution.py:20
  27.1 136.6 %all-reduce.4.cloned.1.call-start = ((), (), s32[]{:S(2)}) async-start(), calls=%async_computation.3 | async-start | bytes 8388608 | tf_op jit(solution)/shard_map/psum | solution.py:31
  67.8 138.8 %all-reduce.6.cloned.1.call-start = ((), (), s32[]{:S(2)}) async-start(), calls=%async_computation.4 | async-start | bytes 8388608 | tf_op jit(solution)/shard_map/psum | solution.py:31
  206.6 17.9 %copy-start.1 = (s32[8]{0:T(128)S(1)}, s32[8]{0:T(128)}, u32[]{:S(2)}) copy-start(s32[8]{0:T(128)} %param.6) | copy-start | bytes 100
  215.1 26.0 %all-to-all-start.1 = ((f32[32,1,4096]{2,1,0:T(1,128)}), f32[32,1,4096]{2,1,0:T(1,128)S(1)}, u32[]{:S(2)}, u32[]{:S(2)}) async-start(f32[32,1,4096]{2,1,0:T(1,128)} %reshape.21), calls=%async_computation.1 | async-start | bytes 1048576 | tf_op jit(solution)/shard_map/all_to_all | solution.py:20
  224.4 122.1 %all-reduce.8.cloned.1.call-start = ((), (), s32[]{:S(2)}) async-start(), calls=%async_computation.5 | async-start | bytes 8388608 | tf_op jit(solution)/shard_map/psum | solution.py:68
  387.4 5.6 %copy-start = (f32[64,16384]{1,0:T(8,128)S(1)}, f32[64,16384]{1,0:T(8,128)}, u32[]{:S(2)}) copy-start(f32[64,16384]{1,0:T(8,128)} %all-reduce.8.cloned.1.call-done) | copy-start | bytes 12582916
Sparse Core Ops, SparseCore 0:
  67.9 95.7 all-reduce.3
  166.7 39.8 all-reduce.5
  273.2 73.2 all-reduce.7
where the time goes:
time: 413 us; the launch traced here: 405 us
  waiting for transfers between devices  242 us (59%)
  matrix products  65.1 us (16%)
  other arithmetic  30.6 us (7%)
  blocking collectives  23.7 us (6%)
  starting transfers between devices  21.8 us (5%)
  between operations  16 us (4%)
  local copies, waits for them, and re-layouts  6.37 us (2%)
    psum x2, waiting for transfers between devices, spread(): x = lax.psum(x, axis)  139 us
    psum x1, waiting for transfers between devices, on_device(): blended = lax.psum(term, VARIANT)  73.5 us
    dot_general x74, matrix products, product(): jnp.dot(left, right, precision=highest, preferred_element_type=jnp.float32)  55.4 us
    all_to_all x2, waiting for transfers between devices, from_everyone(): lax.all_to_all(jnp.broadcast_to(x[None], (count, *x.shape)), axis, 0, 0,...  29.5 us
    all_to_all x1, blocking collectives, from_everyone(): lax.all_to_all(jnp.broadcast_to(x[None], (count, *x.shape)), axis, 0, 0,...  23.7 us
    all_to_all x2, starting transfers between devices, from_everyone(): lax.all_to_all(jnp.broadcast_to(x[None], (count, *x.shape)), axis, 0, 0,...  21.4 us
    another operation x1, matrix products, on_device(): jax.scipy.linalg.solve_triangular(lower_own, own_snap, lower=True)  9.3 us
  transfers between devices with their start and end apart: 5, of which 5 were waited for; matrix products, arithmetic and copies ran while one was open for 0% of the time, Pallas kernels for 0%

commit v1 on v0

v1 whole, which is shorter than its diff:
```python
import functools
import math

import jax
import jax.numpy as jnp
from jax import lax
from jax.experimental import pallas as pl
from jax.experimental.pallas import tpu as pltpu
from jax.sharding import PartitionSpec as P

MESH = pl.DeviceIdType.MESH
HIGHEST = lax.Precision.HIGHEST
K = 64
V = 8
HALF = K // 2
atan_coeffs = [(-1.0) ** k / (2 * k + 1) for k in range(24)]
cos_coeffs = [(-1.0) ** k / math.factorial(2 * k) for k in range(24)]
sin_coeffs = [(-1.0) ** k / math.factorial(2 * k + 1) for k in range(24)]
NEWTON_STEPS = 5
NEWTON_START = 2.0 / (1.0 + 1.0 / 1.64)


def dot(left, right, contract=((1,), (0,))):
    return lax.dot_general(
        left, right, (contract, ((), ())), precision=HIGHEST, preferred_element_type=jnp.float32
    )


NT = ((1,), (1,))


def identity():
    rows = lax.broadcasted_iota(jnp.int32, (K, K), 0)
    columns = lax.broadcasted_iota(jnp.int32, (K, K), 1)
    return jnp.where(rows == columns, 1.0, 0.0).astype(jnp.float32)


def pack(square):
    return jnp.concatenate([square[:HALF], square[HALF:]], axis=1)


def unpack(packed):
    return jnp.concatenate([packed[:, :K], packed[:, K:]], axis=0)


def powers(matrix):
    second = dot(matrix, matrix)
    third = dot(second, matrix)
    fourth = dot(second, second)
    return [
        identity(), matrix, second, third, fourth,
        dot(fourth, matrix), dot(fourth, second), dot(fourth, third), dot(fourth, fourth),
    ]


def group(power, coeffs):
    total = coeffs[0] * power[0]
    for i in range(1, len(coeffs)):
        total = total + coeffs[i] * power[i]
    return total


def series(power, coeffs):
    high = group(power, coeffs[16:24])
    middle = group(power, coeffs[8:16]) + dot(power[8], high)
    return group(power, coeffs[0:8]) + dot(power[8], middle)


def inverse_factor(gram):
    rows = lax.broadcasted_iota(jnp.int32, (K, 2 * K), 0)
    columns = lax.broadcasted_iota(jnp.int32, (K, 2 * K), 1)
    top = lax.broadcasted_iota(jnp.int32, (1, 2 * K), 1)

    def step(j, both):
        row = jnp.sum(jnp.where(rows == j, both, 0.0), axis=0, keepdims=True)
        column = jnp.sum(jnp.where(columns == j, both, 0.0), axis=1, keepdims=True)
        pivot = jnp.sum(jnp.where(top == j, row, 0.0), axis=1, keepdims=True)
        return both - jnp.where(rows > j, column, 0.0) * (row / pivot)

    both = lax.fori_loop(0, K, step, jnp.concatenate([gram, identity()], axis=1))
    pivots = jnp.sum(jnp.where(rows == columns, both, 0.0), axis=1, keepdims=True)
    return both[:, K:] * (1.0 / jnp.sqrt(pivots))


def kernel(
    sizes, root_ref, codes_ref, snap_ref, out_ref,
    own, stack_a, stack_b, ends, made,
    gram_y, gram_z, factors, cross_out, cross_x, cross_y, cross_z, terms, energy_x, energy_y, energy_z,
    sent, got, local,
):
    size_z, size_y, chunk, cols_a, cols_b, scale = sizes
    me = lax.axis_index("variant")
    place = lax.axis_index("mesh")
    chip, core = me // 2, lax.rem(me, 2)
    z, y = place // size_y, lax.rem(place, size_y)
    count = iter(range(1000))

    def variant(dx, dc):
        return lax.rem(chip + dx, 4) * 2 + lax.rem(core + dc, 2)

    x_order = [(2, 0), (2, 1), (1, 0), (3, 0), (1, 1), (3, 1), (0, 1)]
    to_x = [{"variant": variant(dx, dc)} for dx, dc in x_order]
    to_y = [{"mesh": z * size_y + lax.rem(y + d, size_y)} for d in range(1, size_y)]
    to_z = [{"mesh": lax.rem(z + d, size_z) * size_y + y} for d in range(1, size_z)]

    def send(source, target, device):
        i = next(count)
        copy = pltpu.make_async_remote_copy(
            src_ref=source, dst_ref=target, send_sem=sent.at[i], recv_sem=got.at[i],
            device_id=device, device_id_type=MESH,
        )
        copy.start()
        return copy

    def share(buffer, slot, value, devices):
        buffer[slot] = value
        return [send(buffer.at[slot], buffer.at[slot], device) for device in devices]

    def total(buffer, copies):
        for copy in copies:
            copy.wait()
        result = buffer[0]
        for i in range(1, buffer.shape[0]):
            result = result + buffer[i]
        return result

    own_copy = pltpu.make_async_copy(snap_ref, own, local.at[0])
    own_copy.start()
    mine = pl.multiple_of(me * chunk, chunk)
    keep_a = pltpu.make_async_copy(
        snap_ref.at[:, pl.ds(mine, cols_a)], stack_a.at[me], local.at[1]
    )
    keep_b = pltpu.make_async_copy(
        snap_ref.at[:, pl.ds(pl.multiple_of(mine + cols_a, 128), cols_b)], stack_b.at[me], local.at[2]
    )
    keep_a.start()
    keep_b.start()

    barrier = pltpu.get_barrier_semaphore()
    for device in to_x + to_y + to_z:
        pl.semaphore_signal(barrier, inc=1, device_id=device, device_id_type=MESH)
    pl.semaphore_wait(barrier, len(to_x) + len(to_y) + len(to_z))

    stage_a = []
    for device in to_x:
        first = pl.multiple_of(device["variant"] * chunk, chunk)
        stage_a.append(send(snap_ref.at[:, pl.ds(first, cols_a)], stack_a.at[me], device))

    own_copy.wait()

    def gram_step(i, gram):
        block = own[:, pl.ds(pl.multiple_of(i * chunk, chunk), chunk)]
        return gram + dot(block, block, NT)

    gram = lax.fori_loop(0, V, gram_step, jnp.zeros((K, K), jnp.float32))
    gram = total(gram_y, share(gram_y, y, pack(gram), to_y))
    gram = total(gram_z, share(gram_z, z, gram, to_z))
    factor = inverse_factor(unpack(gram))
    factor_copies = share(factors, me, pack(factor), to_x)

    stage_b = []
    for device in to_x:
        first = pl.multiple_of(device["variant"] * chunk + cols_a, 128)
        stage_b.append(send(snap_ref.at[:, pl.ds(first, cols_b)], stack_b.at[me], device))

    for copy in factor_copies:
        copy.wait()
    root = root_ref[0]
    root_factor = unpack(factors[root])
    keep_a.wait()
    keep_b.wait()
    for copy in stage_a:
        copy.wait()
    root_a = stack_a[root]
    cross = dot(root_a, stack_a[...].reshape(V * K, cols_a), NT)
    ends[me, :K, :cols_a] = root_a
    for copy in stage_b:
        copy.wait()
    root_b = stack_b[root]
    cross = cross + dot(root_b, stack_b[...].reshape(V * K, cols_b), NT)
    ends[me, :K, cols_a:] = root_b
    for v in range(V):
        cross_out[v] = pack(cross[:, v * K : (v + 1) * K])
    cross_x[me] = cross_out[me]
    cross_copies = [
        send(cross_out.at[device["variant"]], cross_x.at[me], device) for device in to_x
    ]

    ahead, behind, beside = variant(1, 0), variant(3, 0), variant(0, 1)

    def gather_start(row):
        upper, lower, both = pl.ds(row, HALF), pl.ds(row + HALF, HALF), pl.ds(row, K)
        copies = []
        for rows, device in [(upper, ahead), (lower, behind), (lower, ahead), (upper, behind), (both, beside)]:
            part = ends.at[me, rows]
            copies.append(send(part, part, {"variant": device}))
        return copies

    def gather_relay(row, copies):
        for first, rows, origin, device in [
            (copies[0], pl.ds(row, HALF), behind, ahead),
            (copies[1], pl.ds(row + HALF, HALF), ahead, behind),
        ]:
            first.wait_recv()
            part = ends.at[origin, rows]
            copies.append(send(part, part, {"variant": device}))

    def gather_beside(row, copies, needs, origin):
        for i in needs:
            copies[i].wait_recv()
        part = ends.at[origin, pl.ds(row, K)]
        copies.append(send(part, part, {"variant": beside}))

    roots = gather_start(0)
    cross = total(cross_x, cross_copies)
    cross = total(cross_y, share(cross_y, y, cross, to_y))
    cross_copies = share(cross_z, z, cross, to_z)
    gather_relay(0, roots)
    cross = unpack(total(cross_z, cross_copies))

    projection = dot(dot(root_factor, cross), factor, NT)
    flipped = projection.T
    eye = identity()
    inverse = NEWTON_START * projection
    for _ in range(NEWTON_STEPS):
        inverse = dot(inverse, 2.0 * eye - dot(flipped, inverse))
    tangent_gram = dot(inverse, inverse, NT) - eye
    codes = [codes_ref[v] for v in range(V)]
    own_code = jnp.full((K, K), codes_ref[me], jnp.int32).astype(jnp.float32)
    weight = own_code / jnp.full((K, K), sum(codes[1:], codes[0]), jnp.int32).astype(jnp.float32)
    bend = weight * series(powers(tangent_gram), atan_coeffs)
    turn = dot(bend, dot(inverse, factor))
    term_copies = share(terms, me, jnp.concatenate([turn, bend], axis=1), to_x)
    gather_beside(0, roots, (2,), behind)
    gather_beside(0, roots, (3,), ahead)
    gather_beside(0, roots, (5, 6), variant(2, 0))
    for copy in term_copies:
        copy.wait()
    bends = terms[0, :, K:]
    for v in range(1, V):
        bends = bends + terms[v, :, K:]
    back = dot(bends, root_factor)
    mixer = jnp.concatenate(
        [terms[v, :, :K] - jnp.where(root == v, back, 0.0) for v in range(V)], axis=1
    )
    blended_a = dot(mixer, stack_a[...].reshape(V * K, cols_a))
    ends[me, K:, :cols_a] = blended_a
    blended_b = dot(mixer, stack_b[...].reshape(V * K, cols_b))
    ends[me, K:, cols_a:] = blended_b
    energy = dot(blended_a, blended_a, NT) + dot(blended_b, blended_b, NT)
    energy_copies = share(energy_x, me, pack(energy), to_x)
    blends = gather_start(K)
    energy = total(energy_x, energy_copies)
    energy_copies = share(energy_y, y, energy, to_y)
    energy = total(energy_y, energy_copies)
    energy_copies = share(energy_z, z, energy, to_z)
    gather_relay(K, blends)
    energy = unpack(total(energy_z, energy_copies))
    power = powers(energy)
    final = scale * jnp.concatenate(
        [dot(series(power, cos_coeffs), root_factor), series(power, sin_coeffs)], axis=1
    )

    stores = []

    def finish(v):
        made[v] = dot(final, ends[v])
        columns = pl.ds(pl.multiple_of(v * chunk, chunk), chunk)
        store = pltpu.make_async_copy(made.at[v], out_ref.at[:, columns], local.at[3 + len(stores)])
        store.start()
        stores.append(store)

    for i in (4, 7, 8, 9):
        roots[i].wait_recv()
    finish(me)
    gather_beside(K, blends, (2,), behind)
    gather_beside(K, blends, (3,), ahead)
    blends[4].wait_recv()
    finish(beside)
    finish(behind)
    finish(ahead)
    gather_beside(K, blends, (5, 6), variant(2, 0))
    finish(variant(2, 0))
    blends[7].wait_recv()
    finish(variant(3, 1))
    blends[8].wait_recv()
    finish(variant(1, 1))
    blends[9].wait_recv()
    finish(variant(2, 1))
    for copy in roots + blends:
        copy.wait_send()
    for store in stores:
        store.wait()


def on_device(size_z, size_y, snapshots, ref_index, weight_codes):
    snap = snapshots[0]
    rows = snap.shape[1]
    chunk = rows // V
    cols_a = max(128, chunk * 11 // 16 // 128 * 128)
    cols_b = chunk - cols_a
    sizes = (size_z, size_y, chunk, cols_a, cols_b, math.sqrt(rows * size_z * size_y))
    small = (HALF, 2 * K)
    f32 = jnp.float32
    vmem = [
        (K, rows), (V, K, cols_a), (V, K, cols_b), (V, 2 * K, chunk), (V, K, chunk),
        (size_y, *small), (size_z, *small), (V, *small),
        (V, *small), (V, *small), (size_y, *small), (size_z, *small),
        (V, K, 2 * K), (V, *small), (size_y, *small), (size_z, *small),
    ]
    return pl.pallas_call(
        functools.partial(kernel, sizes),
        out_shape=jax.ShapeDtypeStruct((K, rows), f32),
        in_specs=[
            pl.BlockSpec(memory_space=pltpu.SMEM),
            pl.BlockSpec(memory_space=pltpu.SMEM),
            pl.BlockSpec(memory_space=pl.ANY),
        ],
        out_specs=pl.BlockSpec(memory_space=pl.ANY),
        scratch_shapes=[pltpu.VMEM(shape, f32) for shape in vmem]
        + [
            pltpu.SemaphoreType.DMA((100,)),
            pltpu.SemaphoreType.DMA((100,)),
            pltpu.SemaphoreType.DMA((11,)),
        ],
        compiler_params=pltpu.CompilerParams(
            collective_id=0, has_side_effects=True, vmem_limit_bytes=40 << 20
        ),
        name="interpolate",
    )(ref_index, weight_codes, snap)


def solution(mesh, size_y=4):
    size_z = mesh.shape["mesh"] // size_y
    placed = (P("variant", None, "mesh"), P(), P())
    return jax.shard_map(
        functools.partial(on_device, size_z, size_y),
        mesh=mesh, in_specs=placed, out_specs=P(None, "mesh"), check_vma=False,
    )
```

time: 413 us -> 120 us (0.29); the launches traced: 405 us -> 120 us
  waiting for transfers between devices: 242 us -> 0 us
  Pallas kernels: 0 us -> 114 us
  matrix products: 65.1 us -> 0 us
  other arithmetic: 30.6 us -> 0 us
  blocking collectives: 23.7 us -> 0 us
  starting transfers between devices: 21.8 us -> 0 us
  between operations: 16 us -> 0.67 us
    psum x3 -> x0, waiting for transfers between devices: 212 us -> none  [the longest x2 139 us: spread(): x = lax.psum(x, axis)]
    pallas_call x0 -> x1, Pallas kernels: none -> 114 us  [on_device(): pl.pallas_call(functools.partial(kernel, sizes), out_shape=jax.ShapeDtype...]
    dot_general x74 -> x0, matrix products: 55.4 us -> none  [product(): jnp.dot(left, right, precision=highest, preferred_element_type=jnp.float32)]
    all_to_all x2 -> x0, waiting for transfers between devices: 29.5 us -> none  [from_everyone(): lax.all_to_all(jnp.broadcast_to(x[None], (count, *x.shape)), axis, 0, 0,...]
    another operation x10 -> x0, other arithmetic: 24.1 us -> none  [the longest x3 6.52 us: on_device(): lower_own = jnp.linalg.cholesky(gram_own)]
    all_to_all x1 -> x0, blocking collectives: 23.7 us -> none  [from_everyone(): lax.all_to_all(jnp.broadcast_to(x[None], (count, *x.shape)), axis, 0, 0,...]
    all_to_all x2 -> x0, starting transfers between devices: 21.4 us -> none  [from_everyone(): lax.all_to_all(jnp.broadcast_to(x[None], (count, *x.shape)), axis, 0, 0,...]
    another operation x3 -> x0, matrix products: 9.71 us -> none  [the longest x1 9.3 us: on_device(): jax.scipy.linalg.solve_triangular(lower_own, own_snap, lower=True)]
  transfers between devices with their start and end apart: 5 -> 0, of which waited for: 5 -> 0; matrix products, arithmetic and copies ran while one was open for 0% -> 0% of each run, Pallas kernels for 0% -> 0%
where the time goes in v1:
time: 120 us
  Pallas kernels  114 us (95%)
  local copies, waits for them, and re-layouts  4.85 us (4%)
    pallas_call x1, Pallas kernels, on_device(): pl.pallas_call(functools.partial(kernel, sizes), out_shape=jax.ShapeDtype...  114 us
    unnamed x5, local copies, waits for them, and re-layouts  4.85 us

profile of v1, /device:TPU:1, one launch (start us, length us, event | category | flops | bytes accessed | tf_op | source)
XLA Modules:
  0.0 119.5 jit_solution(15497972766749521051)
XLA Ops:
  0.7 0.0 copy-start
  0.7 2.2 %copy-done = f32[1,64,16384]{2,1,0:T(8,128)S(1)} copy-done((f32[1,64,16384]{2,1,0:T(8,128)S(1)}, f32[1,64,16384]{2,1,0:T(8,128)}, u32[]{:S(2)}) %copy-start) | copy-done | bytes 4194328
  2.8 0.0 copy-start.1
  2.8 0.7 copy-done.1
  3.5 114.0 %interpolate.1 = f32[64,16384]{1,0:T(8,128)S(1)} custom-call(s32[1]{0:T(128)S(6)} %copy.5.root_ref, s32[8]{0:T(128)S(1)} %copy-done.1, f32[64,16384]{1,0:T(8,128)S(1)} %bitcast.1), custom_call_target="tpu_custom_call" | custom-call | tf_op jit(solution)/shard_map/interpolate/pallas_call | solution.py:311
  117.5 2.0 %copy.6 = f32[64,16384]{1,0:T(8,128)} copy(f32[64,16384]{1,0:T(8,128)S(1)} %interpolate.1) | data formatting | bytes 8388608
Async XLA Ops:
  0.7 2.2 %copy-start = (f32[1,64,16384]{2,1,0:T(8,128)S(1)}, f32[1,64,16384]{2,1,0:T(8,128)}, u32[]{:S(2)}) copy-start(f32[1,64,16384]{2,1,0:T(8,128)} %param.3) | copy-start | bytes 12582916
  2.8 0.7 copy-start.1

commit v2 on v1

--- a/solution.py
+++ b/solution.py
@@ -16,8 +16,7 @@
 atan_coeffs = [(-1.0) ** k / (2 * k + 1) for k in range(24)]
 cos_coeffs = [(-1.0) ** k / math.factorial(2 * k) for k in range(24)]
 sin_coeffs = [(-1.0) ** k / math.factorial(2 * k + 1) for k in range(24)]
-NEWTON_STEPS = 5
-NEWTON_START = 2.0 / (1.0 + 1.0 / 1.64)
+MIDDLE = 2.0 / (1.0 + 1.0 / 1.64)
 
 
 def dot(left, right, contract=((1,), (0,))):
@@ -88,7 +87,7 @@
     gram_y, gram_z, factors, cross_out, cross_x, cross_y, cross_z, terms, energy_x, energy_y, energy_z,
     sent, got, local,
 ):
-    size_z, size_y, chunk, cols_a, cols_b, scale = sizes
+    size_z, size_y, chunk, cols_a, cols_b, cols_early, scale = sizes
     me = lax.axis_index("variant")
     place = lax.axis_index("mesh")
     chip, core = me // 2, lax.rem(me, 2)
@@ -146,6 +145,11 @@
         first = pl.multiple_of(device["variant"] * chunk, chunk)
         stage_a.append(send(snap_ref.at[:, pl.ds(first, cols_a)], stack_a.at[me], device))
 
+    stage_b = []
+    for device in to_x:
+        first = pl.multiple_of(device["variant"] * chunk + cols_a, 128)
+        stage_b.append(send(snap_ref.at[:, pl.ds(first, cols_b)], stack_b.at[me], device))
+
     own_copy.wait()
 
     def gram_step(i, gram):
@@ -158,82 +162,89 @@
     factor = inverse_factor(unpack(gram))
     factor_copies = share(factors, me, pack(factor), to_x)
 
-    stage_b = []
-    for device in to_x:
-        first = pl.multiple_of(device["variant"] * chunk + cols_a, 128)
-        stage_b.append(send(snap_ref.at[:, pl.ds(first, cols_b)], stack_b.at[me], device))
-
-    for copy in factor_copies:
-        copy.wait()
-    root = root_ref[0]
-    root_factor = unpack(factors[root])
+    ahead, behind, beside, across = variant(1, 0), variant(3, 0), variant(0, 1), variant(2, 0)
+
+    def gather_start(row, columns):
+        upper, lower, both = pl.ds(row, HALF), pl.ds(row + HALF, HALF), pl.ds(row, K)
+        copies = []
+        for rows, device in [(upper, ahead), (lower, behind), (lower, ahead), (upper, behind), (both, beside)]:
+            part = ends.at[me, rows, columns]
+            copies.append(send(part, part, {"variant": device}))
+        return copies
+
+    def gather_relay(row, columns, copies):
+        for first, rows, origin, device in [
+            (copies[0], pl.ds(row, HALF), behind, ahead),
+            (copies[1], pl.ds(row + HALF, HALF), ahead, behind),
+        ]:
+            first.wait_recv()
+            part = ends.at[origin, rows, columns]
+            copies.append(send(part, part, {"variant": device}))
+
+    def gather_beside(row, groups, needs, origin):
+        for copies in groups:
+            for i in needs:
+                copies[i].wait_recv()
+        part = ends.at[origin, pl.ds(row, K)]
+        return send(part, part, {"variant": beside})
+
+    part_a, part_b = pl.ds(0, cols_early), pl.ds(cols_early, chunk - cols_early)
+
     keep_a.wait()
     keep_b.wait()
     for copy in stage_a:
         copy.wait()
+    root = root_ref[0]
     root_a = stack_a[root]
+    ends[me, :K, :cols_a] = root_a
+    roots_a = gather_start(0, part_a)
     cross = dot(root_a, stack_a[...].reshape(V * K, cols_a), NT)
-    ends[me, :K, :cols_a] = root_a
     for copy in stage_b:
         copy.wait()
     root_b = stack_b[root]
     cross = cross + dot(root_b, stack_b[...].reshape(V * K, cols_b), NT)
-    ends[me, :K, cols_a:] = root_b
     for v in range(V):
         cross_out[v] = pack(cross[:, v * K : (v + 1) * K])
     cross_x[me] = cross_out[me]
     cross_copies = [
         send(cross_out.at[device["variant"]], cross_x.at[me], device) for device in to_x
     ]
-
-    ahead, behind, beside = variant(1, 0), variant(3, 0), variant(0, 1)
-
-    def gather_start(row):
-        upper, lower, both = pl.ds(row, HALF), pl.ds(row + HALF, HALF), pl.ds(row, K)
-        copies = []
-        for rows, device in [(upper, ahead), (lower, behind), (lower, ahead), (upper, behind), (both, beside)]:
-            part = ends.at[me, rows]
-            copies.append(send(part, part, {"variant": device}))
-        return copies
-
-    def gather_relay(row, copies):
-        for first, rows, origin, device in [
-            (copies[0], pl.ds(row, HALF), behind, ahead),
-            (copies[1], pl.ds(row + HALF, HALF), ahead, behind),
-        ]:
-            first.wait_recv()
-            part = ends.at[origin, rows]
-            copies.append(send(part, part, {"variant": device}))
-
-    def gather_beside(row, copies, needs, origin):
-        for i in needs:
-            copies[i].wait_recv()
-        part = ends.at[origin, pl.ds(row, K)]
-        copies.append(send(part, part, {"variant": beside}))
-
-    roots = gather_start(0)
+    ends[me, :K, cols_a:] = root_b
+    roots_b = gather_start(0, part_b)
     cross = total(cross_x, cross_copies)
-    cross = total(cross_y, share(cross_y, y, cross, to_y))
+    cross_copies = share(cross_y, y, cross, to_y)
+    gather_relay(0, part_a, roots_a)
+    cross = total(cross_y, cross_copies)
     cross_copies = share(cross_z, z, cross, to_z)
-    gather_relay(0, roots)
+    gather_relay(0, part_b, roots_b)
+    for copy in factor_copies:
+        copy.wait()
+    root_factor = unpack(factors[root])
     cross = unpack(total(cross_z, cross_copies))
 
     projection = dot(dot(root_factor, cross), factor, NT)
-    flipped = projection.T
     eye = identity()
-    inverse = NEWTON_START * projection
-    for _ in range(NEWTON_STEPS):
-        inverse = dot(inverse, 2.0 * eye - dot(flipped, inverse))
-    tangent_gram = dot(inverse, inverse, NT) - eye
+    rest = eye - MIDDLE * dot(projection, projection, NT)
+    rest_2 = dot(rest, rest)
+    rest_4 = dot(rest_2, rest_2)
+    rest_8 = dot(rest_4, rest_4)
+    inverse = eye + rest
+    for rest in (rest_2, rest_4, rest_8):
+        inverse = inverse + dot(inverse, rest)
+    inverse = MIDDLE * inverse
+    tangent_gram = inverse - eye
+    turn = dot(inverse, dot(projection, factor))
     codes = [codes_ref[v] for v in range(V)]
     own_code = jnp.full((K, K), codes_ref[me], jnp.int32).astype(jnp.float32)
     weight = own_code / jnp.full((K, K), sum(codes[1:], codes[0]), jnp.int32).astype(jnp.float32)
     bend = weight * series(powers(tangent_gram), atan_coeffs)
-    turn = dot(bend, dot(inverse, factor))
+    turn = dot(bend, turn)
     term_copies = share(terms, me, jnp.concatenate([turn, bend], axis=1), to_x)
-    gather_beside(0, roots, (2,), behind)
-    gather_beside(0, roots, (3,), ahead)
-    gather_beside(0, roots, (5, 6), variant(2, 0))
+    roots = [
+        gather_beside(0, (roots_a, roots_b), (2,), behind),
+        gather_beside(0, (roots_a, roots_b), (3,), ahead),
+        gather_beside(0, (roots_a, roots_b), (5, 6), across),
+    ]
     for copy in term_copies:
         copy.wait()
     bends = terms[0, :, K:]
@@ -243,18 +254,23 @@
     mixer = jnp.concatenate(
         [terms[v, :, :K] - jnp.where(root == v, back, 0.0) for v in range(V)], axis=1
     )
-    blended_a = dot(mixer, stack_a[...].reshape(V * K, cols_a))
-    ends[me, K:, :cols_a] = blended_a
-    blended_b = dot(mixer, stack_b[...].reshape(V * K, cols_b))
-    ends[me, K:, cols_a:] = blended_b
-    energy = dot(blended_a, blended_a, NT) + dot(blended_b, blended_b, NT)
+    blended_a = dot(mixer, stack_a[:, :, :cols_early].reshape(V * K, cols_early))
+    ends[me, K:, :cols_early] = blended_a
+    blends_a = gather_start(K, part_a)
+    blended_b = dot(mixer, stack_a[:, :, cols_early:].reshape(V * K, cols_a - cols_early))
+    ends[me, K:, cols_early:cols_a] = blended_b
+    blended_c = dot(mixer, stack_b[...].reshape(V * K, cols_b))
+    ends[me, K:, cols_a:] = blended_c
+    energy = dot(blended_a, blended_a, NT)
+    energy = energy + dot(blended_b, blended_b, NT) + dot(blended_c, blended_c, NT)
     energy_copies = share(energy_x, me, pack(energy), to_x)
-    blends = gather_start(K)
+    blends_b = gather_start(K, part_b)
     energy = total(energy_x, energy_copies)
     energy_copies = share(energy_y, y, energy, to_y)
+    gather_relay(K, part_a, blends_a)
     energy = total(energy_y, energy_copies)
     energy_copies = share(energy_z, z, energy, to_z)
-    gather_relay(K, blends)
+    gather_relay(K, part_b, blends_b)
     energy = unpack(total(energy_z, energy_copies))
     power = powers(energy)
     final = scale * jnp.concatenate(
@@ -270,24 +286,22 @@
         store.start()
         stores.append(store)
 
-    for i in (4, 7, 8, 9):
-        roots[i].wait_recv()
+    groups = (blends_a, blends_b)
+    for copy in [roots_a[4], roots_b[4], *roots]:
+        copy.wait_recv()
     finish(me)
-    gather_beside(K, blends, (2,), behind)
-    gather_beside(K, blends, (3,), ahead)
-    blends[4].wait_recv()
+    blends = [gather_beside(K, groups, (2,), behind), gather_beside(K, groups, (3,), ahead)]
+    for copies in groups:
+        copies[4].wait_recv()
     finish(beside)
     finish(behind)
     finish(ahead)
-    gather_beside(K, blends, (5, 6), variant(2, 0))
-    finish(variant(2, 0))
-    blends[7].wait_recv()
-    finish(variant(3, 1))
-    blends[8].wait_recv()
-    finish(variant(1, 1))
-    blends[9].wait_recv()
-    finish(variant(2, 1))
-    for copy in roots + blends:
+    blends.append(gather_beside(K, groups, (5, 6), across))
+    finish(across)
+    for copy, dx in zip(blends, (3, 1, 2)):
+        copy.wait_recv()
+        finish(variant(dx, 1))
+    for copy in roots_a + roots_b + roots + blends_a + blends_b + blends:
         copy.wait_send()
     for store in stores:
         store.wait()
@@ -299,7 +313,8 @@
     chunk = rows // V
     cols_a = max(128, chunk * 11 // 16 // 128 * 128)
     cols_b = chunk - cols_a
-    sizes = (size_z, size_y, chunk, cols_a, cols_b, math.sqrt(rows * size_z * size_y))
+    cols_early = max(128, chunk // 4 // 128 * 128)
+    sizes = (size_z, size_y, chunk, cols_a, cols_b, cols_early, math.sqrt(rows * size_z * size_y))
     small = (HALF, 2 * K)
     f32 = jnp.float32
     vmem = [
@@ -314,20 +329,20 @@
         in_specs=[
             pl.BlockSpec(memory_space=pltpu.SMEM),
             pl.BlockSpec(memory_space=pltpu.SMEM),
-            pl.BlockSpec(memory_space=pl.ANY),
+            pl.BlockSpec(memory_space=pltpu.HBM),
         ],
         out_specs=pl.BlockSpec(memory_space=pl.ANY),
         scratch_shapes=[pltpu.VMEM(shape, f32) for shape in vmem]
         + [
-            pltpu.SemaphoreType.DMA((100,)),
-            pltpu.SemaphoreType.DMA((100,)),
+            pltpu.SemaphoreType.DMA((120,)),
+            pltpu.SemaphoreType.DMA((120,)),
             pltpu.SemaphoreType.DMA((11,)),
         ],
         compiler_params=pltpu.CompilerParams(
             collective_id=0, has_side_effects=True, vmem_limit_bytes=40 << 20
         ),
         name="interpolate",
-    )(ref_index, weight_codes, snap)
+    )(ref_index, weight_codes, pltpu.with_memory_space_constraint(snap, pltpu.HBM))
 
 
 def solution(mesh, size_y=4):

time: 120 us -> 112 us (0.933)
  Pallas kernels: 114 us -> 109 us
  local copies, waits for them, and re-layouts: 4.85 us -> 2.66 us
    pallas_call x1, Pallas kernels: 114 us -> 109 us  [on_device(): pl.pallas_call(functools.partial(kernel, sizes), out_shape=jax.ShapeDtype...]
    unnamed x5 -> x3, local copies, waits for them, and re-layouts: 4.85 us -> 2.66 us
where the time goes in v2:
time: 112 us
  Pallas kernels  109 us (97%)
  local copies, waits for them, and re-layouts  2.66 us (2%)
    pallas_call x1, Pallas kernels, on_device(): pl.pallas_call(functools.partial(kernel, sizes), out_shape=jax.ShapeDtype...  109 us
    unnamed x3, local copies, waits for them, and re-layouts  2.66 us

profile of v2, /device:TPU:1, one launch (start us, length us, event | category | flops | bytes accessed | tf_op | source)
XLA Modules:
  0.0 112.3 jit_solution(7916138504781261807)
XLA Ops:
  0.7 0.0 copy-start
  0.7 0.6 copy-done
  1.3 109.0 %interpolate.1 = f32[64,16384]{1,0:T(8,128)S(1)} custom-call(s32[1]{0:T(128)S(6)} %copy.5.root_ref, s32[8]{0:T(128)S(1)} %copy-done, f32[64,16384]{1,0:T(8,128)} %bitcast.1), custom_call_target="tpu_custom_call" | custom-call | tf_op jit(solution)/shard_map/interpolate/pallas_call | solution.py:326
  110.3 2.0 %copy.6 = f32[64,16384]{1,0:T(8,128)} copy(f32[64,16384]{1,0:T(8,128)S(1)} %interpolate.1) | data formatting | bytes 8388608
Async XLA Ops:
  0.7 0.7 copy-start

commit v3 on v2

--- a/solution.py
+++ b/solution.py
@@ -26,6 +26,25 @@
 
 
 NT = ((1,), (1,))
+NN = ((1,), (0,))
+
+
+def split(array):
+    high = array.astype(jnp.bfloat16)
+    return high, (array - high.astype(jnp.float32)).astype(jnp.bfloat16)
+
+
+def split_dot(left, high, low, contract):
+    rows = left.shape[0]
+    left_high, left_low = split(left)
+    both = lax.dot_general(
+        jnp.concatenate([left_high, left_low], axis=0), high, (contract, ((), ())),
+        preferred_element_type=jnp.float32,
+    )
+    other = lax.dot_general(
+        left_high, low, (contract, ((), ())), preferred_element_type=jnp.float32
+    )
+    return both[:rows] + (both[rows:] + other)
 
 
 def identity():
@@ -85,7 +104,7 @@
     sizes, root_ref, codes_ref, snap_ref, out_ref,
     own, stack_a, stack_b, ends, made,
     gram_y, gram_z, factors, cross_out, cross_x, cross_y, cross_z, terms, energy_x, energy_y, energy_z,
-    sent, got, local,
+    high_a, low_a, high_b, low_b, sent, got, local,
 ):
     size_z, size_y, chunk, cols_a, cols_b, cols_early, scale = sizes
     me = lax.axis_index("variant")
@@ -198,11 +217,13 @@
     root_a = stack_a[root]
     ends[me, :K, :cols_a] = root_a
     roots_a = gather_start(0, part_a)
-    cross = dot(root_a, stack_a[...].reshape(V * K, cols_a), NT)
+    high_a[...], low_a[...] = split(stack_a[...].reshape(V * K, cols_a))
+    cross = split_dot(root_a, high_a[...], low_a[...], NT)
     for copy in stage_b:
         copy.wait()
     root_b = stack_b[root]
-    cross = cross + dot(root_b, stack_b[...].reshape(V * K, cols_b), NT)
+    high_b[...], low_b[...] = split(stack_b[...].reshape(V * K, cols_b))
+    cross = cross + split_dot(root_b, high_b[...], low_b[...], NT)
     for v in range(V):
         cross_out[v] = pack(cross[:, v * K : (v + 1) * K])
     cross_x[me] = cross_out[me]
@@ -254,15 +275,16 @@
     mixer = jnp.concatenate(
         [terms[v, :, :K] - jnp.where(root == v, back, 0.0) for v in range(V)], axis=1
     )
-    blended_a = dot(mixer, stack_a[:, :, :cols_early].reshape(V * K, cols_early))
+    blended_a = split_dot(mixer, high_a[:, :cols_early], low_a[:, :cols_early], NN)
     ends[me, K:, :cols_early] = blended_a
     blends_a = gather_start(K, part_a)
-    blended_b = dot(mixer, stack_a[:, :, cols_early:].reshape(V * K, cols_a - cols_early))
+    blended_b = split_dot(mixer, high_a[:, cols_early:], low_a[:, cols_early:], NN)
     ends[me, K:, cols_early:cols_a] = blended_b
-    blended_c = dot(mixer, stack_b[...].reshape(V * K, cols_b))
+    blended_c = split_dot(mixer, high_b[...], low_b[...], NN)
     ends[me, K:, cols_a:] = blended_c
-    energy = dot(blended_a, blended_a, NT)
-    energy = energy + dot(blended_b, blended_b, NT) + dot(blended_c, blended_c, NT)
+    energy = jnp.zeros((K, K), jnp.float32)
+    for blended in (blended_a, blended_b, blended_c):
+        energy = energy + split_dot(blended, *split(blended), NT)
     energy_copies = share(energy_x, me, pack(energy), to_x)
     blends_b = gather_start(K, part_b)
     energy = total(energy_x, energy_copies)
@@ -272,6 +294,8 @@
     energy_copies = share(energy_z, z, energy, to_z)
     gather_relay(K, part_b, blends_b)
     energy = unpack(total(energy_z, energy_copies))
+    groups = (blends_a, blends_b)
+    blends = [gather_beside(K, groups, (2,), behind), gather_beside(K, groups, (3,), ahead)]
     power = powers(energy)
     final = scale * jnp.concatenate(
         [dot(series(power, cos_coeffs), root_factor), series(power, sin_coeffs)], axis=1
@@ -280,27 +304,27 @@
     stores = []
 
     def finish(v):
-        made[v] = dot(final, ends[v])
+        made[v] = split_dot(final, *split(ends[v]), NN)
         columns = pl.ds(pl.multiple_of(v * chunk, chunk), chunk)
         store = pltpu.make_async_copy(made.at[v], out_ref.at[:, columns], local.at[3 + len(stores)])
         store.start()
         stores.append(store)
 
-    groups = (blends_a, blends_b)
     for copy in [roots_a[4], roots_b[4], *roots]:
         copy.wait_recv()
     finish(me)
-    blends = [gather_beside(K, groups, (2,), behind), gather_beside(K, groups, (3,), ahead)]
+    finish(behind)
+    finish(ahead)
     for copies in groups:
         copies[4].wait_recv()
     finish(beside)
-    finish(behind)
-    finish(ahead)
+    for copy, dx in zip(blends, (3, 1)):
+        copy.wait_recv()
+        finish(variant(dx, 1))
     blends.append(gather_beside(K, groups, (5, 6), across))
     finish(across)
-    for copy, dx in zip(blends, (3, 1, 2)):
-        copy.wait_recv()
-        finish(variant(dx, 1))
+    blends[2].wait_recv()
+    finish(variant(2, 1))
     for copy in roots_a + roots_b + roots + blends_a + blends_b + blends:
         copy.wait_send()
     for store in stores:
@@ -311,9 +335,9 @@
     snap = snapshots[0]
     rows = snap.shape[1]
     chunk = rows // V
-    cols_a = max(128, chunk * 11 // 16 // 128 * 128)
+    cols_a = max(256, chunk * 13 // 16 // 128 * 128)
     cols_b = chunk - cols_a
-    cols_early = max(128, chunk // 4 // 128 * 128)
+    cols_early = max(128, chunk // 8 // 128 * 128)
     sizes = (size_z, size_y, chunk, cols_a, cols_b, cols_early, math.sqrt(rows * size_z * size_y))
     small = (HALF, 2 * K)
     f32 = jnp.float32
@@ -333,6 +357,7 @@
         ],
         out_specs=pl.BlockSpec(memory_space=pl.ANY),
         scratch_shapes=[pltpu.VMEM(shape, f32) for shape in vmem]
+        + [pltpu.VMEM((V * K, cols), jnp.bfloat16) for cols in (cols_a, cols_a, cols_b, cols_b)]
         + [
             pltpu.SemaphoreType.DMA((120,)),
             pltpu.SemaphoreType.DMA((120,)),

time: 112 us -> 109 us (0.973)
  Pallas kernels: 109 us -> 106 us
    pallas_call x1, Pallas kernels: 109 us -> 106 us  [on_device(): pl.pallas_call(functools.partial(kernel, sizes), out_shape=jax.ShapeDtype...]
where the time goes in v3:
time: 109 us
  Pallas kernels  106 us (97%)
  local copies, waits for them, and re-layouts  2.66 us (2%)
    pallas_call x1, Pallas kernels, on_device(): pl.pallas_call(functools.partial(kernel, sizes), out_shape=jax.ShapeDtype...  106 us
    unnamed x3, local copies, waits for them, and re-layouts  2.66 us

profile of v3, /device:TPU:1, one launch (start us, length us, event | category | flops | bytes accessed | tf_op | source)
XLA Modules:
  0.0 109.4 jit_solution(13928236969774481578)
XLA Ops:
  0.7 0.0 copy-start
  0.7 0.6 copy-done
  1.3 106.0 %interpolate.1 = f32[64,16384]{1,0:T(8,128)S(1)} custom-call(s32[1]{0:T(128)S(6)} %copy.5.root_ref, s32[8]{0:T(128)S(1)} %copy-done, f32[64,16384]{1,0:T(8,128)} %bitcast.1), custom_call_target="tpu_custom_call" | custom-call | tf_op jit(solution)/shard_map/interpolate/pallas_call | solution.py:350
  107.3 2.0 %copy.6 = f32[64,16384]{1,0:T(8,128)} copy(f32[64,16384]{1,0:T(8,128)S(1)} %interpolate.1) | data formatting | bytes 8388608
Async XLA Ops:
  0.7 0.7 copy-start

commit v4 on v3

--- a/solution.py
+++ b/solution.py
@@ -179,9 +179,10 @@
     gram = total(gram_y, share(gram_y, y, pack(gram), to_y))
     gram = total(gram_z, share(gram_z, z, gram, to_z))
     factor = inverse_factor(unpack(gram))
-    factor_copies = share(factors, me, pack(factor), to_x)
-
     ahead, behind, beside, across = variant(1, 0), variant(3, 0), variant(0, 1), variant(2, 0)
+    factor_copies = share(
+        factors, me, pack(factor), [{"variant": v} for v in (across, ahead, behind, beside)]
+    )
 
     def gather_start(row, columns):
         upper, lower, both = pl.ds(row, HALF), pl.ds(row + HALF, HALF), pl.ds(row, K)
@@ -200,14 +201,16 @@
             part = ends.at[origin, rows, columns]
             copies.append(send(part, part, {"variant": device}))
 
-    def gather_beside(row, groups, needs, origin):
+    def gather_beside(row, groups, needs, origin, columns):
         for copies in groups:
             for i in needs:
                 copies[i].wait_recv()
-        part = ends.at[origin, pl.ds(row, K)]
+        part = ends.at[origin, pl.ds(row, K), columns]
         return send(part, part, {"variant": beside})
 
-    part_a, part_b = pl.ds(0, cols_early), pl.ds(cols_early, chunk - cols_early)
+    whole = pl.ds(0, chunk)
+    part_a, part_b = pl.ds(0, chunk // 4), pl.ds(chunk // 4, chunk // 2)
+    root_last = pl.ds(chunk - chunk // 4, chunk // 4)
 
     keep_a.wait()
     keep_b.wait()
@@ -232,14 +235,20 @@
     ]
     ends[me, :K, cols_a:] = root_b
     roots_b = gather_start(0, part_b)
+    roots_c = gather_start(0, root_last)
     cross = total(cross_x, cross_copies)
     cross_copies = share(cross_y, y, cross, to_y)
+    factor_relays = []
+    for copy, origin in zip(factor_copies, (across, behind, ahead)):
+        copy.wait_recv()
+        factor_relays.append(send(factors.at[origin], factors.at[origin], {"variant": beside}))
     gather_relay(0, part_a, roots_a)
     cross = total(cross_y, cross_copies)
     cross_copies = share(cross_z, z, cross, to_z)
     gather_relay(0, part_b, roots_b)
-    for copy in factor_copies:
-        copy.wait()
+    gather_relay(0, root_last, roots_c)
+    for copy in factor_copies[3:] + factor_relays:
+        copy.wait_recv()
     root_factor = unpack(factors[root])
     cross = unpack(total(cross_z, cross_copies))
 
@@ -261,11 +270,6 @@
     bend = weight * series(powers(tangent_gram), atan_coeffs)
     turn = dot(bend, turn)
     term_copies = share(terms, me, jnp.concatenate([turn, bend], axis=1), to_x)
-    roots = [
-        gather_beside(0, (roots_a, roots_b), (2,), behind),
-        gather_beside(0, (roots_a, roots_b), (3,), ahead),
-        gather_beside(0, (roots_a, roots_b), (5, 6), across),
-    ]
     for copy in term_copies:
         copy.wait()
     bends = terms[0, :, K:]
@@ -275,6 +279,8 @@
     mixer = jnp.concatenate(
         [terms[v, :, :K] - jnp.where(root == v, back, 0.0) for v in range(V)], axis=1
     )
+    part_a, part_b = pl.ds(0, cols_early), pl.ds(cols_early, cols_a - cols_early)
+    part_c = pl.ds(cols_a, cols_b)
     blended_a = split_dot(mixer, high_a[:, :cols_early], low_a[:, :cols_early], NN)
     ends[me, K:, :cols_early] = blended_a
     blends_a = gather_start(K, part_a)
@@ -287,45 +293,62 @@
         energy = energy + split_dot(blended, *split(blended), NT)
     energy_copies = share(energy_x, me, pack(energy), to_x)
     blends_b = gather_start(K, part_b)
+    blends_c = gather_start(K, part_c)
+    root_groups = (roots_a, roots_b, roots_c)
+    roots = [
+        gather_beside(0, root_groups, (2,), behind, whole),
+        gather_beside(0, root_groups, (3,), ahead, whole),
+    ]
     energy = total(energy_x, energy_copies)
     energy_copies = share(energy_y, y, energy, to_y)
     gather_relay(K, part_a, blends_a)
+    roots.append(gather_beside(0, root_groups, (5, 6), across, whole))
     energy = total(energy_y, energy_copies)
     energy_copies = share(energy_z, z, energy, to_z)
     gather_relay(K, part_b, blends_b)
     energy = unpack(total(energy_z, energy_copies))
-    groups = (blends_a, blends_b)
-    blends = [gather_beside(K, groups, (2,), behind), gather_beside(K, groups, (3,), ahead)]
     power = powers(energy)
     final = scale * jnp.concatenate(
         [dot(series(power, cos_coeffs), root_factor), series(power, sin_coeffs)], axis=1
     )
 
+    gather_relay(K, part_c, blends_c)
+    groups = (blends_a, blends_b, blends_c)
+    blends = [
+        gather_beside(K, groups, (2,), behind, whole), gather_beside(K, groups, (3,), ahead, whole)
+    ]
     stores = []
 
-    def finish(v):
-        made[v] = split_dot(final, *split(ends[v]), NN)
-        columns = pl.ds(pl.multiple_of(v * chunk, chunk), chunk)
-        store = pltpu.make_async_copy(made.at[v], out_ref.at[:, columns], local.at[3 + len(stores)])
+    def finish(v, first, columns):
+        part = pl.ds(first, columns)
+        made[v, :, part] = split_dot(final, *split(ends[v, :, part]), NN)
+        target = out_ref.at[:, pl.ds(pl.multiple_of(v * chunk + first, 128), columns)]
+        store = pltpu.make_async_copy(made.at[v, :, part], target, local.at[3 + len(stores)])
         store.start()
         stores.append(store)
 
-    for copy in [roots_a[4], roots_b[4], *roots]:
+    for copy in [roots_a[4], roots_b[4], roots_c[4], *roots]:
         copy.wait_recv()
-    finish(me)
-    finish(behind)
-    finish(ahead)
+    finish(me, 0, chunk)
+    finish(behind, 0, chunk)
+    finish(ahead, 0, chunk)
     for copies in groups:
         copies[4].wait_recv()
-    finish(beside)
+    finish(beside, 0, chunk)
+    early, late = pl.ds(0, cols_a), part_c
     for copy, dx in zip(blends, (3, 1)):
         copy.wait_recv()
-        finish(variant(dx, 1))
-    blends.append(gather_beside(K, groups, (5, 6), across))
-    finish(across)
+        finish(variant(dx, 1), 0, chunk)
+    blends.append(gather_beside(K, groups[:2], (5, 6), across, early))
+    finish(across, 0, cols_a)
+    blends.append(gather_beside(K, groups[2:], (5, 6), across, late))
+    finish(across, cols_a, cols_b)
     blends[2].wait_recv()
-    finish(variant(2, 1))
-    for copy in roots_a + roots_b + roots + blends_a + blends_b + blends:
+    finish(variant(2, 1), 0, cols_a)
+    blends[3].wait_recv()
+    finish(variant(2, 1), cols_a, cols_b)
+    gathers = roots_a + roots_b + roots_c + roots + blends_a + blends_b + blends_c + blends
+    for copy in factor_copies + factor_relays + gathers:
         copy.wait_send()
     for store in stores:
         store.wait()
@@ -359,15 +382,15 @@
         scratch_shapes=[pltpu.VMEM(shape, f32) for shape in vmem]
         + [pltpu.VMEM((V * K, cols), jnp.bfloat16) for cols in (cols_a, cols_a, cols_b, cols_b)]
         + [
-            pltpu.SemaphoreType.DMA((120,)),
-            pltpu.SemaphoreType.DMA((120,)),
-            pltpu.SemaphoreType.DMA((11,)),
+            pltpu.SemaphoreType.DMA((160,)),
+            pltpu.SemaphoreType.DMA((160,)),
+            pltpu.SemaphoreType.DMA((16,)),
         ],
         compiler_params=pltpu.CompilerParams(
             collective_id=0, has_side_effects=True, vmem_limit_bytes=40 << 20
         ),
         name="interpolate",
-    )(ref_index, weight_codes, pltpu.with_memory_space_constraint(snap, pltpu.HBM))
+    )(ref_index, pltpu.with_memory_space_constraint(weight_codes, pltpu.HBM), pltpu.with_memory_space_constraint(snap, pltpu.HBM))
 
 
 def solution(mesh, size_y=4):

time: 109 us -> 108 us (level)
    unnamed x3 -> x1, local copies, waits for them, and re-layouts: 2.66 us -> 2.02 us
where the time goes in v4:
time: 108 us
  Pallas kernels  105 us (97%)
  local copies, waits for them, and re-layouts  2.02 us (2%)
    pallas_call x1, Pallas kernels, on_device(): pl.pallas_call(functools.partial(kernel, sizes), out_shape=jax.ShapeDtype...  105 us

profile of v4, /device:TPU:1, one launch (start us, length us, event | category | flops | bytes accessed | tf_op | source)
XLA Modules:
  0.0 107.9 jit_solution(14544336188702893163)
XLA Ops:
  0.7 105.2 %interpolate.1 = f32[64,16384]{1,0:T(8,128)S(1)} custom-call(s32[1]{0:T(128)S(6)} %copy.5.root_ref, s32[8]{0:T(128)} %codes_ref.1, f32[64,16384]{1,0:T(8,128)} %bitcast.1), custom_call_target="tpu_custom_call" | custom-call | tf_op jit(solution)/shard_map/interpolate/pallas_call | solution.py:373
  105.9 2.0 %copy.6 = f32[64,16384]{1,0:T(8,128)} copy(f32[64,16384]{1,0:T(8,128)S(1)} %interpolate.1) | data formatting | bytes 8388608

commit v5 on v4

--- a/solution.py
+++ b/solution.py
@@ -291,7 +291,9 @@
     energy = jnp.zeros((K, K), jnp.float32)
     for blended in (blended_a, blended_b, blended_c):
         energy = energy + split_dot(blended, *split(blended), NT)
-    energy_copies = share(energy_x, me, pack(energy), to_x)
+    energy_copies = share(
+        energy_x, me, pack(energy), [{"variant": v} for v in (across, ahead, behind, beside)]
+    )
     blends_b = gather_start(K, part_b)
     blends_c = gather_start(K, part_c)
     root_groups = (roots_a, roots_b, roots_c)
@@ -299,7 +301,12 @@
         gather_beside(0, root_groups, (2,), behind, whole),
         gather_beside(0, root_groups, (3,), ahead, whole),
     ]
-    energy = total(energy_x, energy_copies)
+    for copy, origin in zip(energy_copies[:3], (across, behind, ahead)):
+        copy.wait_recv()
+        energy_copies.append(send(energy_x.at[origin], energy_x.at[origin], {"variant": beside}))
+    for copy in energy_copies[:3]:
+        copy.wait_send()
+    energy = total(energy_x, energy_copies[3:])
     energy_copies = share(energy_y, y, energy, to_y)
     gather_relay(K, part_a, blends_a)
     roots.append(gather_beside(0, root_groups, (5, 6), across, whole))

time: 108 us -> 108 us (level)
  no operation moved by 1% of the time
where the time goes in v5:
time: 108 us
  Pallas kernels  105 us (97%)
  local copies, waits for them, and re-layouts  2.02 us (2%)
    pallas_call x1, Pallas kernels, on_device(): pl.pallas_call(functools.partial(kernel, sizes), out_shape=jax.ShapeDtype...  105 us

profile of v5, /device:TPU:1, one launch (start us, length us, event | category | flops | bytes accessed | tf_op | source)
XLA Modules:
  0.0 107.7 jit_solution(17158373315047213331)
XLA Ops:
  0.7 105.0 %interpolate.1 = f32[64,16384]{1,0:T(8,128)S(1)} custom-call(s32[1]{0:T(128)S(6)} %copy.5.root_ref, s32[8]{0:T(128)} %codes_ref.1, f32[64,16384]{1,0:T(8,128)} %bitcast.1), custom_call_target="tpu_custom_call" | custom-call | tf_op jit(solution)/shard_map/interpolate/pallas_call | solution.py:380
  105.7 2.0 %copy.6 = f32[64,16384]{1,0:T(8,128)} copy(f32[64,16384]{1,0:T(8,128)S(1)} %interpolate.1) | data formatting | bytes 8388608

commit v6 on v5

--- a/solution.py
+++ b/solution.py
@@ -313,13 +313,13 @@
     energy = total(energy_y, energy_copies)
     energy_copies = share(energy_z, z, energy, to_z)
     gather_relay(K, part_b, blends_b)
+    gather_relay(K, part_c, blends_c)
     energy = unpack(total(energy_z, energy_copies))
     power = powers(energy)
     final = scale * jnp.concatenate(
         [dot(series(power, cos_coeffs), root_factor), series(power, sin_coeffs)], axis=1
     )
 
-    gather_relay(K, part_c, blends_c)
     groups = (blends_a, blends_b, blends_c)
     blends = [
         gather_beside(K, groups, (2,), behind, whole), gather_beside(K, groups, (3,), ahead, whole)

time: 108 us -> 107 us (level)
  no operation moved by 1% of the time
where the time goes in v6:
time: 107 us
  Pallas kernels  105 us (98%)
  local copies, waits for them, and re-layouts  2.02 us (2%)
    pallas_call x1, Pallas kernels, on_device(): pl.pallas_call(functools.partial(kernel, sizes), out_shape=jax.ShapeDtype...  105 us

profile of v6, /device:TPU:1, one launch (start us, length us, event | category | flops | bytes accessed | tf_op | source)
XLA Modules:
  0.0 107.2 jit_solution(18030539798418607184)
XLA Ops:
  0.7 104.5 %interpolate.1 = f32[64,16384]{1,0:T(8,128)S(1)} custom-call(s32[1]{0:T(128)S(6)} %copy.5.root_ref, s32[8]{0:T(128)} %codes_ref.1, f32[64,16384]{1,0:T(8,128)} %bitcast.1), custom_call_target="tpu_custom_call" | custom-call | tf_op jit(solution)/shard_map/interpolate/pallas_call | solution.py:380
  105.2 2.0 %copy.6 = f32[64,16384]{1,0:T(8,128)} copy(f32[64,16384]{1,0:T(8,128)S(1)} %interpolate.1) | data formatting | bytes 8388608
